TPU v7x, 32 devices: a whole 2x2x4 slice. The times are simulated.
32 devices in a mesh: var: 8 (over y, x, core), tp: 4 (over z).
Axes of the slice: x: 2, y: 2, z: 4, core: 2. Of those that a mesh axis runs over, the one named last changes fastest.
Arguments:
- projected: bfloat16 [64, 32, 3, 8192], P(('var', 'tp')), may hold values from -6 to 6
- cache_history: bfloat16 [48, 127, 8192], P('var', None, 'tp'), may hold values from -6 to 6
- cache_inputs: bfloat16 [48, 6, 3, 8192], P('var', None, None, 'tp'), may hold values from -6 to 6
- feature_taps: bfloat16 [7, 3, 8192], P(None, None, 'tp'), may hold values from -2 to 2
- filters: bfloat16 [128, 512], P(None, 'tp'), may hold values from -0.5 to 0.5
- skip_weight: bfloat16 [8192], P('tp'), may hold values from -4 to 4
- base_inputs: bfloat16 [4, 3, 8192], P(None, None, 'tp'), may hold values from -6 to 6
- window_owner: int32 [64, 1], replicated, may hold values from 0 to 7; in each aligned block of 8 rows (0 to 7, 8 to 15, ...) at most 2 rows name the same one
- window_slot: int32 [64], replicated, may hold values from 0 to 5
- variant_position: int32 [64], P('var'), may hold values from 0 to 31
- allele: int32 [64], P('var'), may hold values from 0 to 3
Outputs:
- mixer_out: bfloat16 [64, 32, 8192], P(('var', 'tp'))
Inputs may be any that keep to these rules, and one draw needn't show every extreme that they name: `window_owner`: among the windows of one index of var (aligned blocks of 8 rows), at most 2 name the same owner.
All inputs are finite; a program needn't handle non-finite values.
Results may differ from a plain program's by a relative error of at most 0.0049.
Values may be sent and summed in bfloat16 or wider, within the bound.
A program may use at most 128 MiB of HBM per device.

v0:
```python
import jax
import jax.numpy as jnp
from jax import lax
from jax.sharding import PartitionSpec as P


def tap_table(filters, row_count, col_count, offset):
    tap_count = filters.shape[0]
    lag_index = jnp.arange(row_count)[:, None] + offset - jnp.arange(col_count)[None, :]
    onehot = (lag_index[:, :, None] == jnp.arange(tap_count)[None, None, :]).astype(jnp.bfloat16)
    return jnp.einsum("tsj,jg->gts", onehot, filters, preferred_element_type=jnp.float32).astype(
        jnp.bfloat16
    )


def apply_table(table, values, group_size):
    item_count, length, channel_width = values.shape
    grouped = values.reshape(item_count, length, channel_width // group_size, group_size)
    result = jnp.einsum("gts,nsgc->ntgc", table, grouped, preferred_element_type=jnp.float32)
    return result.reshape(item_count, table.shape[1], channel_width)


def featurize(extended, feature_taps, window_len):
    item_count, ext_len, stream_count, channel_width = extended.shape
    wide = stream_count * channel_width
    flat_in = extended.reshape(item_count, ext_len, wide)
    kernel = feature_taps[::-1].reshape(feature_taps.shape[0], 1, wide)
    result = lax.conv_general_dilated(
        flat_in,
        kernel,
        window_strides=(1,),
        padding="VALID",
        dimension_numbers=("NWC", "WIO", "NWC"),
        feature_group_count=wide,
        preferred_element_type=jnp.float32,
    )
    return result.reshape(item_count, window_len, stream_count, channel_width)


def local(
    projected,
    cache_history,
    cache_inputs,
    feature_taps,
    filters,
    skip_weight,
    base_inputs,
    window_owner,
    window_slot,
    variant_position,
    allele,
):
    var_count = lax.axis_size("var")
    my_index = lax.axis_index("var")
    local_windows = variant_position.shape[0]
    capacity = max(2, 2 * local_windows // var_count)
    window_len = projected.shape[1]
    history_len = cache_history.shape[1]
    channel_width = cache_history.shape[2]
    group_size = channel_width // filters.shape[1]
    owners_all = window_owner[:, 0].reshape(var_count, local_windows)
    slots_all = window_slot.reshape(var_count, local_windows)
    same_owner = (
        owners_all[:, :, None] == jnp.arange(var_count, dtype=jnp.int32)[None, None, :]
    ).astype(jnp.int32)
    earlier = jnp.cumsum(same_owner, axis=1) - same_owner
    rank_all = jnp.sum(earlier * same_owner, axis=2)
    matches = (owners_all[:, None, :] == my_index) & (
        rank_all[:, None, :] == jnp.arange(capacity, dtype=jnp.int32)[None, :, None]
    )
    slot_pick = jnp.sum(jnp.where(matches, slots_all[:, None, :], 0), axis=2).reshape(-1)
    own_owner = lax.dynamic_index_in_dim(owners_all, my_index, 0, keepdims=False)
    own_rank = lax.dynamic_index_in_dim(rank_all, my_index, 0, keepdims=False)
    source_row = own_owner * capacity + own_rank
    lead_send = jnp.take(cache_inputs, slot_pick, axis=0).reshape(
        (var_count, capacity) + cache_inputs.shape[1:]
    )
    carry_rows = min(window_len, history_len)
    table_pre = tap_table(filters, carry_rows, history_len, history_len)
    owned = apply_table(table_pre, cache_history, group_size).astype(jnp.bfloat16)
    carry_send = jnp.take(owned, slot_pick, axis=0).reshape(
        var_count, capacity, carry_rows, channel_width
    )
    carry_got, lead_got = (
        lax.all_to_all(carry_send, "var", split_axis=0, concat_axis=0, tiled=True),
        lax.all_to_all(lead_send, "var", split_axis=0, concat_axis=0, tiled=True),
    )
    carried = jnp.take(
        carry_got.reshape(var_count * capacity, carry_rows, channel_width), source_row, axis=0
    )
    lead_mine = jnp.take(
        lead_got.reshape((var_count * capacity,) + lead_got.shape[2:]), source_row, axis=0
    )
    channels = lax.all_to_all(projected, "tp", split_axis=3, concat_axis=0, tiled=True)
    allele_hot = (allele[:, None] == jnp.arange(base_inputs.shape[0])[None, :]).astype(jnp.bfloat16)
    base_rows = jnp.einsum(
        "wb,bsc->wsc", allele_hot, base_inputs, preferred_element_type=jnp.float32
    ).astype(jnp.bfloat16)
    placed = jnp.arange(window_len)[None, :] == variant_position[:, None]
    altered = jnp.where(placed[:, :, None, None], base_rows[:, None], channels)
    extended = jnp.concatenate([lead_mine, altered], axis=1)
    featured = featurize(extended, feature_taps, window_len)
    mixed_in = lax.optimization_barrier(
        (featured[:, :, 1] * featured[:, :, 2]).astype(jnp.bfloat16)
    )
    table_win = tap_table(filters, window_len, window_len, 0)
    inside = apply_table(table_win, mixed_in, group_size)
    filtered = (
        inside
        + carried.astype(jnp.float32)
        + skip_weight.astype(jnp.float32) * mixed_in.astype(jnp.float32)
    )
    mixer_out = (featured[:, :, 0] * filtered).astype(jnp.bfloat16)
    return lax.all_to_all(mixer_out, "tp", split_axis=0, concat_axis=2, tiled=True)


def solution(mesh):
    return jax.shard_map(
        local,
        mesh=mesh,
        in_specs=(
            P(("var", "tp"), None, None, None),
            P("var", None, "tp"),
            P("var", None, None, "tp"),
            P(None, None, "tp"),
            P(None, "tp"),
            P("tp"),
            P(None, None, "tp"),
            P(),
            P(),
            P("var"),
            P("var"),
        ),
        out_specs=P(("var", "tp"), None, None),
        check_vma=False,
    )
```

profile of v0, /device:TPU:0, one launch (start us, length us, event | category | flops | bytes accessed | tf_op | source)
XLA Modules:
  0.0 271.2 jit_solution(2574274719932674839)
XLA Ops:
  9.6 5.2 %all-to-all-start = ((bf16[8,2,6,3,2048]{4,1,3,2,0:T(2,128)(2,1)}), bf16[8,2,6,3,2048]{4,1,3,2,0:T(2,128)(2,1)}, u32[]{:S(2)}, u32[]{:S(2)}) async-start(bf16[8,2,6,3,2048]{4,1,3,2,0:T(2,128)(2,1)} %copy.78), calls=%async_computation | async-start | bytes 2359296 | tf_op jit(solution)/shard_map/all_to_all | solution.py:86
  16.8 4.7 %copy.93 = bf16[6,127,2048]{1,2,0:T(8,128)(2,1)} copy(bf16[6,127,2048]{2,1,0:T(8,128)(2,1)} %param.12) | data formatting | bytes 6242304 | tf_op args[1]
  21.5 2.4 copy.95
  27.8 6.5 %gather_fusion.2 = bf16[16,32,2048]{1,2,0:T(8,128)(2,1)} fusion(bf16[6,32,2048]{1,2,0:T(8,128)(2,1)} %bitcast.73, s32[1024]{0:T(1024)S(1)} %pad_clamp_fusion.1), kind=kCustom, calls=%fused_computation.2 | custom fusion | bytes 4194368 | tf_op jit(solution)/shard_map/jit(_take)/gather | solution.py:81
  34.3 6.7 %copy.97 = bf16[8,2,32,2048]{3,2,1,0:T(8,128)(2,1)S(1)} copy(bf16[8,2,32,2048]{2,3,1,0:T(8,128)(2,1)} %bitcast.70) | data formatting | bytes 4194304 | tf_op jit(solution)/shard_map/jit(_take)/gather | solution.py:81
  42.7 4.2 %all-to-all-start.2 = ((bf16[8,2,32,2048]{3,2,1,0:T(8,128)(2,1)}), bf16[8,2,32,2048]{3,2,1,0:T(8,128)(2,1)S(1)}, u32[]{:S(2)}, u32[]{:S(2)}) async-start(bf16[8,2,32,2048]{3,2,1,0:T(8,128)(2,1)} %broadcast_select_fusion.1), calls=%async_computation.2 | async-start | bytes 4194304 | tf_op jit(solution)/shard_map/all_to_all | solution.py:85
  46.9 20.0 %copy.81 = bf16[2,32,3,8192]{1,2,0,3:T(4,128)(2,1)} copy(bf16[2,32,3,8192]{3,1,2,0:T(8,128)(2,1)} %param.11) | data formatting | bytes 6291456 | tf_op args[0]
  66.9 14.1 %reshape.243 = bf16[4,2,196608]{2,1,0:T(2,128)(2,1)} reshape(bf16[8192,2,3,32]{3,2,1,0:T(4,128)(2,1)} %bitcast.65) | data formatting | bytes 6291456
  81.0 5.4 %all-to-all-start.1 = ((bf16[4,2,196608]{2,1,0:T(2,128)(2,1)}), bf16[4,2,196608]{2,1,0:T(2,128)(2,1)}, u32[]{:S(2)}, u32[]{:S(2)}) async-start(bf16[4,2,196608]{2,1,0:T(2,128)(2,1)} %reshape.243), calls=%async_computation.1 | async-start | bytes 6291456 | tf_op jit(solution)/shard_map/all_to_all | solution.py:94
  86.5 5.0 %rev.3 = bf16[7,3,2048]{2,0,1:T(8,128)(2,1)} reverse(bf16[7,3,2048]{2,0,1:T(8,128)(2,1)S(1)} %copy-done.6), dimensions={0} | reverse | bytes 172032 | tf_op jit(solution)/shard_map/rev | solution.py:27
  91.8 2.3 copy.100
  95.0 3.0 %copy.79 = bf16[8,2,6,3,2048]{4,2,3,1,0:T(8,128)(2,1)} copy(bf16[8,2,6,3,2048]{4,1,3,2,0:T(2,128)(2,1)} %all-to-all-done) | data formatting | bytes 2359296 | tf_op jit(solution)/shard_map/all_to_all | solution.py:86
  102.0 55.9 %all-to-all-done.1 = bf16[4,2,196608]{2,1,0:T(2,128)(2,1)} async-done(((bf16[4,2,196608]{2,1,0:T(2,128)(2,1)}), bf16[4,2,196608]{2,1,0:T(2,128)(2,1)}, u32[]{:S(2)}, u32[]{:S(2)}) %all-to-all-start.1) | async-done | bytes 3145760 | tf_op jit(solution)/shard_map/all_to_all | solution.py:94
  157.9 14.1 %reshape.244 = bf16[8192,2,3,32]{3,2,1,0:T(4,128)(2,1)} reshape(bf16[4,2,196608]{2,1,0:T(2,128)(2,1)} %all-to-all-done.1) | data formatting | bytes 6291456
  172.0 25.2 %copy.82 = bf16[2,32,3,4,2048]{4,2,1,0,3:T(4,128)(2,1)} copy(bf16[2,32,3,4,2048]{1,2,0,4,3:T(4,128)(2,1)} %bitcast.64) | data formatting | bytes 6291456 | tf_op jit(solution)/shard_map/all_to_all | solution.py:94
  197.2 9.7 %all_to_all.36 = bf16[8,32,6144]{2,1,0:T(8,128)(2,1)} reshape(bf16[4,2,32,3,2048]{4,3,2,1,0:T(4,128)(2,1)} %bitcast.68) | data formatting | bytes 6291456 | tf_op jit(solution)/shard_map/all_to_all | solution.py:94
  206.9 5.4 %copy_select_fusion = bf16[8,32,6144]{2,0,1:T(8,128)(2,1)S(1)} fusion(bf16[8,32,6144]{2,1,0:T(8,128)(2,1)} %all_to_all.36, pred[8,32]{0,1:T(8,128)(4,1)S(1)} %iota_compare_fusion.9, bf16[8,6144]{1,0:T(8,128)(2,1)S(1)} %bitcast.80), kind=kLoop, calls=%fused_computation.11 | loop fusion | flops 1572864 | bytes 6390016 | tf_op jit(solution)/shard_map/jit(_where)/select_n | solution.py:100
  212.3 4.9 %fusion.2 = f32[8,32,6144]{2,0,1:T(8,128)S(1)} fusion(bf16[8,32,6144]{2,0,1:T(8,128)(2,1)S(1)} %copy_select_fusion, bf16[8,6,6144]{2,0,1:T(8,128)(2,1)S(1)} %broadcast_select_fusion.2, bf16[7,1,6144]{2,0,1:T(8,128)(2,1)S(1)} %bitcast.81), kind=kOutput, calls=%fused_computation.6 | convolution fusion | flops 23887872 | bytes 10113024 | tf_op jit(solution)/shard_map/conv_general_dilated | solution.py:28
  221.5 3.1 %copy.88 = bf16[8,32,2048]{1,2,0:T(8,128)(2,1)} copy(bf16[8,32,2048]{2,1,0:T(8,128)(2,1)S(1)} %fusion.16) | data formatting | bytes 2097152 | tf_op jit(solution)/shard_map/optimization_barrier | solution.py:103
  224.6 3.4 %fusion.6 = f32[8,32,128,16]{1,3,0,2:T(8,128)S(1)} fusion(bf16[128,32,32,1]{2,1,3,0:T(8,128)(2,1)S(1)} %copy-done.3, bf16[8,32,128,16]{1,3,2,0:T(8,128)(2,1)} %bitcast.69), kind=kOutput, calls=%fused_computation.10 | convolution fusion | flops 33554432 | bytes 3407872 | tf_op jit(solution)/shard_map/gts,nsgc->ntgc/dot_general | solution.py:19
  228.1 3.9 %copy.91 = f32[8,32,128,16]{1,3,2,0:T(8,128)} copy(f32[8,32,128,16]{1,3,0,2:T(8,128)S(1)} %fusion.6) | data formatting | bytes 4194304 | tf_op jit(solution)/shard_map/gts,nsgc->ntgc/transpose | solution.py:19
  232.0 6.3 %copy.98 = f32[8,32,2048]{2,1,0:T(8,128)} copy(f32[8,32,2048]{1,2,0:T(8,128)} %bitcast.66) | data formatting | bytes 4194304 | tf_op jit(solution)/shard_map/reshape | solution.py:20
  238.4 3.8 %fusion.11 = bf16[8,32,2048]{2,1,0:T(8,128)(2,1)S(1)} fusion(f32[8,32,1,2048]{3,0,2,1:T(8,128)} %get-tuple-element.8, bf16[8,32,2048]{2,1,0:T(8,128)(2,1)S(1)} %fusion.16, f32[8,32,2048]{2,1,0:T(8,128)} %copy.98, f32[2048]{0:T(1024)S(1)} %convert_element_type.60, bf16[8,32,2048]{2,1,0:T(8,128)(2,1)S(1)} %copy-done.2, pred[8]{0:T(512)(128)(4,1)S(1)} %get-tuple-element.5), kind=kLoop, calls=%fused_computation.19 | loop fusion | flops 4194304 | bytes 7348232 | tf_op jit(solution)/shard_map/convert_element_type | solution.py:113
  242.1 28.0 %all_to_all.46 = bf16[8,32,2048]{2,1,0:T(8,128)(2,1)S(1)} all-to-all(bf16[8,32,2048]{2,1,0:T(8,128)(2,1)S(1)} %fusion.11), channel_id=1, replica_groups=mesh['var'=8,'tp'=4] {'tp'}, dimensions={0} | all-to-all | bytes 2097152 | tf_op jit(solution)/shard_map/all_to_all | solution.py:114
  (67 shorter events, 27.7 us)
Async XLA Ops:
  0.0 3.6 %copy-start = (bf16[6,6,3,2048]{3,2,1,0:T(4,128)(2,1)S(1)}, bf16[6,6,3,2048]{3,2,1,0:T(4,128)(2,1)}, u32[]{:S(2)}) copy-start(bf16[6,6,3,2048]{3,2,1,0:T(4,128)(2,1)} %param.13) | copy-start | bytes 1327108
  7.6 7.3 %copy-start.5 = (bf16[128,128]{1,0:T(8,128)(2,1)S(1)}, bf16[128,128]{1,0:T(8,128)(2,1)}, u32[]{:S(2)}) copy-start(bf16[128,128]{1,0:T(8,128)(2,1)} %param.15) | copy-start | bytes 98308
  9.6 33.1 %all-to-all-start = ((bf16[8,2,6,3,2048]{4,1,3,2,0:T(2,128)(2,1)}), bf16[8,2,6,3,2048]{4,1,3,2,0:T(2,128)(2,1)}, u32[]{:S(2)}, u32[]{:S(2)}) async-start(bf16[8,2,6,3,2048]{4,1,3,2,0:T(2,128)(2,1)} %copy.78), calls=%async_computation | async-start | bytes 2359296 | tf_op jit(solution)/shard_map/all_to_all | solution.py:86
  42.7 38.4 %all-to-all-start.2 = ((bf16[8,2,32,2048]{3,2,1,0:T(8,128)(2,1)}), bf16[8,2,32,2048]{3,2,1,0:T(8,128)(2,1)S(1)}, u32[]{:S(2)}, u32[]{:S(2)}) async-start(bf16[8,2,32,2048]{3,2,1,0:T(8,128)(2,1)} %broadcast_select_fusion.1), calls=%async_computation.2 | async-start | bytes 4194304 | tf_op jit(solution)/shard_map/all_to_all | solution.py:85
  81.0 5.5 %copy-start.6 = (bf16[7,3,2048]{2,0,1:T(8,128)(2,1)S(1)}, bf16[7,3,2048]{2,0,1:T(8,128)(2,1)}, u32[]{:S(2)}) copy-start(bf16[7,3,2048]{2,0,1:T(8,128)(2,1)} %param.14) | copy-start | bytes 258052
  81.0 13.1 %copy-start.9 = (bf16[2048]{0:T(1024)(128)(2,1)S(1)}, bf16[2048]{0:T(1024)(128)(2,1)}, u32[]{:S(2)}) copy-start(bf16[2048]{0:T(1024)(128)(2,1)} %param.16) | copy-start | bytes 12292
  81.0 13.1 %copy-start.11 = (s32[8]{0:T(128)S(1)}, s32[8]{0:T(128)}, u32[]{:S(2)}) copy-start(s32[8]{0:T(128)} %param.20) | copy-start | bytes 100
  81.0 13.1 %copy-start.8 = (bf16[4,3,2048]{2,0,1:T(4,128)(2,1)S(1)}, bf16[4,3,2048]{2,0,1:T(4,128)(2,1)}, u32[]{:S(2)}) copy-start(bf16[4,3,2048]{2,0,1:T(4,128)(2,1)} %param.17) | copy-start | bytes 147460
  81.0 13.1 %copy-start.10 = (s32[8]{0:T(128)S(1)}, s32[8]{0:T(128)}, u32[]{:S(2)}) copy-start(s32[8]{0:T(128)} %param.21) | copy-start | bytes 100
  81.0 76.9 %all-to-all-start.1 = ((bf16[4,2,196608]{2,1,0:T(2,128)(2,1)}), bf16[4,2,196608]{2,1,0:T(2,128)(2,1)}, u32[]{:S(2)}, u32[]{:S(2)}) async-start(bf16[4,2,196608]{2,1,0:T(2,128)(2,1)} %reshape.243), calls=%async_computation.1 | async-start | bytes 6291456 | tf_op jit(solution)/shard_map/all_to_all | solution.py:94
  197.2 9.7 %copy-start.4 = (bf16[8,3,2048]{2,0,1:T(8,128)(2,1)S(1)}, bf16[8,3,2048]{2,0,1:T(8,128)(2,1)}, u32[]{:S(2)}) copy-start(bf16[8,3,2048]{2,0,1:T(8,128)(2,1)} %convolution_convert_fusion) | copy-start | bytes 294916
  206.9 5.4 %copy-start.7 = (bf16[7,3,2048]{2,0,1:T(8,128)(2,1)S(1)}, bf16[7,3,2048]{2,0,1:T(8,128)(2,1)}, u32[]{:S(2)}) copy-start(bf16[7,3,2048]{2,0,1:T(8,128)(2,1)} %rev.3) | copy-start | bytes 258052
  221.5 3.1 %copy-start.3 = (bf16[128,32,32,1]{2,1,3,0:T(8,128)(2,1)S(1)}, bf16[128,32,32,1]{2,1,3,0:T(8,128)(2,1)}, u32[]{:S(2)}) copy-start(bf16[128,32,32,1]{2,1,3,0:T(8,128)(2,1)} %copy.100) | copy-start | bytes 786436
  232.0 6.4 %copy-start.2 = (bf16[8,32,2048]{2,1,0:T(8,128)(2,1)S(1)}, bf16[8,32,2048]{2,1,0:T(8,128)(2,1)}, u32[]{:S(2)}) copy-start(bf16[8,32,2048]{2,1,0:T(8,128)(2,1)} %gather_fusion.3) | copy-start | bytes 3145732
  238.4 32.8 %copy-start.1 = (bf16[6,6,3,2048]{3,2,1,0:T(4,128)(2,1)S(1)}, bf16[6,6,3,2048]{3,2,1,0:T(4,128)(2,1)}, u32[]{:S(2)}) copy-start(bf16[6,6,3,2048]{3,2,1,0:T(4,128)(2,1)} %param.13) | copy-start | bytes 1327108
where the time goes:
time: 273 us; the launch traced here: 271 us
  local copies, waits for them, and re-layouts  143 us (52%)
  waiting for transfers between devices  55.9 us (20%)
  blocking collectives  28 us (10%)
  other arithmetic  17.8 us (7%)
  starting transfers between devices  14.8 us (5%)
  matrix products  11.4 us (4%)
    all_to_all x1, waiting for transfers between devices, local(): lax.all_to_all(projected, 'tp', split_axis=3, concat_axis=0, tiled=True)  55.9 us
    unnamed x29, local copies, waits for them, and re-layouts  53.5 us
    all_to_all x2, local copies, waits for them, and re-layouts, local(): lax.all_to_all(projected, 'tp', split_axis=3, concat_axis=0, tiled=True)  34.9 us
    all_to_all x1, blocking collectives, local(): lax.all_to_all(mixer_out, 'tp', split_axis=0, concat_axis=2, tiled=True)  28 us
    gather x2, local copies, waits for them, and re-layouts, local(): jnp.take(owned, slot_pick, axis=0)  13.2 us
    reshape x1, local copies, waits for them, and re-layouts, apply_table(): return result.reshape(item_count, table.shape[1], channel_width)  6.35 us
  transfers between devices with their start and end apart: 3, of which 1 were waited for; matrix products, arithmetic and copies ran while one was open for 29% of the time, Pallas kernels for 0%

commit v1 on v0

v1 whole, which is shorter than its diff:
```python
import functools

import jax
import jax.numpy as jnp
from jax import lax
from jax.experimental import pallas as pl
from jax.experimental.pallas import tpu as pltpu
from jax.sharding import PartitionSpec as P

LANES = 128
ROWS = 112
F32 = jnp.float32
BF16 = jnp.bfloat16


def skewed(rows, first, keep):
    parts = []
    for g in range(8):
        wide = jnp.broadcast_to(rows[g : g + 1], (32, LANES))
        wide = pltpu.roll(wide, first, 1, stride=1, stride_axis=0)
        parts.append(jnp.where(keep, wide, 0.0))
    return jnp.concatenate(parts, axis=0).astype(BF16)


def own_group(stacked, lane_group):
    out = stacked[0:32]
    for g in range(1, 8):
        out = jnp.where(lane_group == g, stacked[g * 32 : g * 32 + 32], out)
    return out


def kernel(
    n_var, n_tp, chunks, width,
    owner, slot, pos, allele, hist, lead, proj_far, taps, frev, base,
    out,
    owned, proj, all_taps, all_frev, ext, pick, rank,
    s1, r1, l1, s2, r2, l2, sp, rp, lp, lj,
    *blocks,
):
    send1, recv1, send2, recv2 = (blocks[k * chunks : (k + 1) * chunks] for k in range(4))
    slots = hist.shape[0]
    history = hist.shape[1]
    chan = hist.shape[2]
    local = pos.shape[0]
    group = chan // frev.shape[0]
    me = lax.axis_index("var")
    mt = lax.axis_index("tp")

    load_proj = pltpu.make_async_copy(proj_far, proj, lj.at[0])
    load_proj.start()
    barrier = pltpu.get_barrier_semaphore()

    def greet_var(d, _):
        pl.semaphore_signal(barrier, inc=1, device_id={"var": lax.rem(me + d, n_var)}, device_id_type=pl.DeviceIdType.MESH)
        return 0

    def greet_tp(d, _):
        pl.semaphore_signal(barrier, inc=1, device_id={"tp": lax.rem(mt + d, n_tp)}, device_id_type=pl.DeviceIdType.MESH)
        return 0

    lax.fori_loop(1, n_var, greet_var, 0)
    lax.fori_loop(1, n_tp, greet_tp, 0)
    pl.semaphore_wait(barrier, n_var - 1 + n_tp - 1)

    def param_copy(k, d, src, dst, landed, to):
        return pltpu.make_async_remote_copy(
            src_ref=src, dst_ref=dst.at[landed], send_sem=sp.at[k, d], recv_sem=rp.at[k, d],
            device_id={"tp": to}, device_id_type=pl.DeviceIdType.MESH)

    def hop1(q, d, row, landed, to):
        return pltpu.make_async_remote_copy(
            src_ref=send1[q].at[row], dst_ref=recv1[q].at[landed], send_sem=s1.at[q, d], recv_sem=r1.at[q, d],
            device_id={"var": to}, device_id_type=pl.DeviceIdType.MESH)

    def hop2(q, d, row, landed, to):
        return pltpu.make_async_remote_copy(
            src_ref=send2[q].at[row], dst_ref=recv2[q].at[landed], send_sem=s2.at[q, d], recv_sem=r2.at[q, d],
            device_id={"tp": to}, device_id_type=pl.DeviceIdType.MESH)

    def start_params(d, _):
        to = lax.rem(mt + d, n_tp)
        param_copy(0, d, taps, all_taps, mt, to).start()
        param_copy(1, d, frev, all_frev, mt, to).start()
        return 0

    lax.fori_loop(1, n_tp, start_params, 0)
    keep_taps = pltpu.make_async_copy(taps, all_taps.at[mt], lp.at[0])
    keep_frev = pltpu.make_async_copy(frev, all_frev.at[mt], lp.at[1])
    keep_taps.start()
    keep_frev.start()

    def picks(v, _):
        def one(i, state):
            count, first, second = state
            hit = (owner[v * local + i] == me).astype(jnp.int32)
            which = slot[v * local + i]
            first = first + jnp.where(count == 0, hit * which, 0)
            second = second + jnp.where(count == 1, hit * which, 0)
            return count + hit, first, second

        zero = jnp.int32(0)
        _, first, second = lax.fori_loop(0, local, one, (zero, zero, zero))
        pick[2 * v] = first
        pick[2 * v + 1] = second
        return 0

    lax.fori_loop(0, n_var, picks, 0)

    def ranks(w, _):
        def one(i, count):
            same = (owner[me * local + i] == owner[me * local + w]).astype(jnp.int32)
            return count + jnp.where(i < w, same, 0)

        rank[w] = lax.fori_loop(0, local, one, jnp.int32(0))
        return 0

    lax.fori_loop(0, local, ranks, 0)

    row32 = lax.broadcasted_iota(jnp.int32, (32, LANES), 0)
    lane32 = lax.broadcasted_iota(jnp.int32, (32, LANES), 1)
    lane_group = lane32 // group
    upper = lane32 >= row32
    lower = lane32 <= row32
    row16 = lax.broadcasted_iota(jnp.int32, (16, width), 0)
    row8 = lax.broadcasted_iota(jnp.int32, (8, width), 0)
    pairs = width // (2 * LANES)

    def carry_chunk(q):
        def body(b, _):
            at = b * (2 * LANES)
            lanes0 = q * width + at
            rows = frev[pl.ds(pl.multiple_of(lanes0 // group, 16), 16), :].astype(F32)
            for half in range(2):
                table = skewed(rows[half * 8 : half * 8 + 8], 0, upper)[:, :history]
                here = pl.ds(pl.multiple_of(lanes0 + half * LANES, LANES), LANES)
                there = pl.ds(pl.multiple_of(at + half * LANES, LANES), LANES)
                for n in range(slots):
                    got = jnp.dot(table, hist[n, :, here], preferred_element_type=F32)
                    owned[n, :, there] = own_group(got, lane_group).astype(BF16)
            return 0

        lax.fori_loop(0, pairs, body, 0)
        chunk = pl.ds(q * width, width)

        def fill(v, _):
            a, b = pick[2 * v], pick[2 * v + 1]
            send1[q][v, 0:32, :] = owned[a]
            send1[q][v, 32:64, :] = owned[b]
            for s in range(3):
                both = jnp.where(row16 < 8, lead[a, s, :, chunk].astype(F32), lead[b, s, :, chunk].astype(F32))
                send1[q][v, 64 + 16 * s : 80 + 16 * s, :] = both.astype(BF16)
            return 0

        lax.fori_loop(0, n_var, fill, 0)

        def start(d, _):
            to = lax.rem(me + d, n_var)
            hop1(q, d, to, me, to).start()
            return 0

        lax.fori_loop(1, n_var, start, 0)
        pltpu.make_async_copy(send1[q].at[me], recv1[q].at[me], l1.at[q]).start()

    for q in range(chunks):
        carry_chunk(q)

    def finish_params(d, _):
        src = lax.rem(mt + n_tp - d, n_tp)
        to = lax.rem(mt + d, n_tp)
        param_copy(0, d, taps, all_taps, src, to).wait_recv()
        param_copy(1, d, frev, all_frev, src, to).wait_recv()
        param_copy(0, d, taps, all_taps, mt, to).wait_send()
        param_copy(1, d, frev, all_frev, mt, to).wait_send()
        return 0

    lax.fori_loop(1, n_tp, finish_params, 0)
    keep_taps.wait()
    keep_frev.wait()

    def route(q):
        def arrive(d, _):
            hop1(q, d, lax.rem(me + d, n_var), lax.rem(me + n_var - d, n_var), lax.rem(me + d, n_var)).wait_recv()
            return 0

        lax.fori_loop(1, n_var, arrive, 0)
        pltpu.make_async_copy(send1[q].at[me], recv1[q].at[me], l1.at[q]).wait()
        chunk = pl.ds(q * width, width)

        def fill(t, _):
            for i in range(2):
                w = 2 * t + i
                o, r = owner[me * local + w], rank[w]
                send2[q][t, 32 * i : 32 * i + 32, :] = jnp.where(
                    r == 0, recv1[q][o, 0:32, :].astype(F32), recv1[q][o, 32:64, :].astype(F32)
                ).astype(BF16)
            for s in range(3):
                halves = []
                for i in range(2):
                    w = 2 * t + i
                    o, r = owner[me * local + w], rank[w]
                    both = recv1[q][o, 64 + 16 * s : 80 + 16 * s, :].astype(F32)
                    half = jnp.where(r == 0, both[0:8], both[8:16])
                    token = base[allele[w], :, chunk]
                    halves.append(jnp.where(row8 == 0, token[s : s + 1], half))
                send2[q][t, 64 + 16 * s : 80 + 16 * s, :] = jnp.concatenate(halves, axis=0).astype(BF16)
            return 0

        lax.fori_loop(0, n_tp, fill, 0)

        def start(d, _):
            to = lax.rem(mt + d, n_tp)
            hop2(q, d, to, mt, to).start()
            return 0

        lax.fori_loop(1, n_tp, start, 0)
        pltpu.make_async_copy(send2[q].at[mt], recv2[q].at[mt], l2.at[q]).start()

    def mix(q):
        def arrive(d, _):
            hop2(q, d, lax.rem(mt + d, n_tp), lax.rem(mt + n_tp - d, n_tp), lax.rem(mt + d, n_tp)).wait_recv()
            return 0

        lax.fori_loop(1, n_tp, arrive, 0)
        pltpu.make_async_copy(send2[q].at[mt], recv2[q].at[mt], l2.at[q]).wait()

        def body(step, _):
            c = step // pairs
            at = (step % pairs) * (2 * LANES)
            lanes0 = q * width + at
            rows = all_frev[c, pl.ds(pl.multiple_of(lanes0 // group, 16), 16), :].astype(F32)
            for half in range(2):
                table = skewed(rows[half * 8 : half * 8 + 8], 1, lower)[:, :32]
                here = pl.ds(pl.multiple_of(lanes0 + half * LANES, LANES), LANES)
                there = pl.ds(pl.multiple_of(at + half * LANES, LANES), LANES)
                glob = pl.ds(pl.multiple_of(c * chan + lanes0 + half * LANES, LANES), LANES)
                par = all_taps[c, :, here].astype(F32)
                gates, mixes = [], []
                for w in range(2):
                    place = row32 == pos[2 * mt + w]
                    feats = []
                    for s in range(3):
                        k = (half * 2 + w) * 3 + s
                        before = recv2[q][c, 64 + 16 * s : 80 + 16 * s, there].astype(F32)[8 * w : 8 * w + 8]
                        altered = jnp.where(place, before[0:1], proj[w, s, :, glob].astype(F32))
                        ext[k, 0:8, :] = before
                        ext[k, 8:40, :] = altered
                        total = par[8 * s : 8 * s + 1] * altered
                        for j in range(1, 7):
                            total = total + par[8 * s + j : 8 * s + j + 1] * ext[k, 8 - j : 40 - j, :]
                        feats.append(total)
                    gates.append(feats[0])
                    mixes.append((feats[1] * feats[2]).astype(BF16))
                got = jnp.dot(table, jnp.concatenate(mixes, axis=1), preferred_element_type=F32)
                for w in range(2):
                    inside = own_group(got[:, w * LANES : (w + 1) * LANES], lane_group)
                    carried = recv2[q][c, 32 * w : 32 * w + 32, there].astype(F32)
                    filtered = inside + carried + par[24:25] * mixes[w].astype(F32)
                    out[w, :, glob] = (gates[w] * filtered).astype(BF16)
            return 0

        lax.fori_loop(0, n_tp * pairs, body, 0)

    load_proj.wait()
    for q in range(min(2, chunks)):
        route(q)
    for q in range(chunks):
        mix(q)
        if q + 2 < chunks:
            route(q + 2)

    for q in range(chunks):
        def one(d, _, q=q):
            to = lax.rem(me + d, n_var)
            hop1(q, d, to, me, to).wait_send()
            return 0

        def two(d, _, q=q):
            to = lax.rem(mt + d, n_tp)
            hop2(q, d, to, mt, to).wait_send()
            return 0

        lax.fori_loop(1, n_var, one, 0)
        lax.fori_loop(1, n_tp, two, 0)


def local(projected, cache_history, cache_inputs, feature_taps, filters, skip_weight, base_inputs,
          window_owner, window_slot, variant_position, allele):
    n_var, n_tp = lax.axis_size("var"), lax.axis_size("tp")
    slots, history, chan = cache_history.shape
    window_len, full = projected.shape[1], projected.shape[3]
    width = min(512, chan)
    chunks = chan // width
    proj = projected.transpose(0, 2, 1, 3)
    lead = jnp.pad(cache_inputs.transpose(0, 2, 1, 3), ((0, 0), (0, 0), (2, 0), (0, 0)))
    lead = jnp.concatenate([lead, lead], axis=2)
    taps = jnp.pad(feature_taps.transpose(1, 0, 2), ((0, 0), (0, 1), (0, 0))).reshape(24, chan)
    taps = jnp.concatenate([taps, jnp.pad(skip_weight[None], ((0, 7), (0, 0)))], axis=0)
    frev = filters[::-1].T
    base = jnp.pad(base_inputs.astype(F32), ((0, 0), (0, 5), (0, 0)))
    groups = filters.shape[1]
    vm = pl.BlockSpec(memory_space=pltpu.VMEM)
    sm = pl.BlockSpec(memory_space=pltpu.SMEM)
    dma = pltpu.SemaphoreType.DMA
    return pl.pallas_call(
        functools.partial(kernel, n_var, n_tp, chunks, width),
        out_shape=jax.ShapeDtypeStruct((2, window_len, full), BF16),
        in_specs=[sm] * 4 + [vm] * 2 + [pl.BlockSpec(memory_space=pl.ANY)] + [vm] * 3,
        out_specs=vm,
        scratch_shapes=[
            pltpu.VMEM((slots, 32, width), BF16),
            pltpu.VMEM(proj.shape, BF16),
            pltpu.VMEM((n_tp, 32, chan), BF16),
            pltpu.VMEM((n_tp, groups, LANES), BF16),
            pltpu.VMEM((12, 40, LANES), F32),
            pltpu.SMEM((2 * n_var,), jnp.int32),
            pltpu.SMEM((variant_position.shape[0],), jnp.int32),
            dma((chunks, n_var)), dma((chunks, n_var)), dma((chunks,)),
            dma((chunks, n_tp)), dma((chunks, n_tp)), dma((chunks,)),
            dma((2, n_tp)), dma((2, n_tp)), dma((2,)), dma((1,)),
        ]
        + [pltpu.VMEM((n_var, ROWS, width), BF16)] * (2 * chunks)
        + [pltpu.VMEM((n_tp, ROWS, width), BF16)] * (2 * chunks),
        compiler_params=pltpu.CompilerParams(
            collective_id=0, has_side_effects=True, vmem_limit_bytes=48 * 1024 * 1024
        ),
        cost_estimate=pl.CostEstimate(flops=6 * 10**9, bytes_accessed=12 * 10**6, transcendentals=0),
    )(window_owner[:, 0], window_slot, variant_position, allele, cache_history, lead, proj, taps, frev, base)


def solution(mesh):
    return jax.shard_map(
        local,
        mesh=mesh,
        in_specs=(
            P(("var", "tp"), None, None, None),
            P("var", None, "tp"),
            P("var", None, None, "tp"),
            P(None, None, "tp"),
            P(None, "tp"),
            P("tp"),
            P(None, None, "tp"),
            P(),
            P(),
            P("var"),
            P("var"),
        ),
        out_specs=P(("var", "tp"), None, None),
        check_vma=False,
    )
```

time: 273 us -> 71.3 us (0.26)
  local copies, waits for them, and re-layouts: 143 us -> 6.21 us
  Pallas kernels: 0 us -> 64.1 us
  waiting for transfers between devices: 55.9 us -> 0 us
  blocking collectives: 28 us -> 0 us
  other arithmetic: 17.8 us -> 0.18 us
  starting transfers between devices: 14.8 us -> 0 us
  matrix products: 11.4 us -> 0 us
    pallas_call x0 -> x1, Pallas kernels: none -> 64.1 us  [local(): pl.pallas_call(functools.partial(kernel, n_var, n_tp, chunks, width), out...]
    all_to_all x3 -> x0, waiting for transfers between devices: 55.9 us -> none  [the longest x1 55.9 us: local(): lax.all_to_all(projected, 'tp', split_axis=3, concat_axis=0, tiled=True)]
    unnamed x29 -> x14, local copies, waits for them, and re-layouts: 53.5 us -> 4.33 us
    all_to_all x4 -> x0, local copies, waits for them, and re-layouts: 38.9 us -> none  [the longest x2 34.9 us: local(): lax.all_to_all(projected, 'tp', split_axis=3, concat_axis=0, tiled=True)]
    all_to_all x1 -> x0, blocking collectives: 28 us -> none  [local(): lax.all_to_all(mixer_out, 'tp', split_axis=0, concat_axis=2, tiled=True)]
    gather x6 -> x0, local copies, waits for them, and re-layouts: 19 us -> none  [the longest x2 13.2 us: local(): jnp.take(owned, slot_pick, axis=0)]
    all_to_all x3 -> x0, starting transfers between devices: 14.8 us -> none  [the longest x1 5.44 us: local(): lax.all_to_all(projected, 'tp', split_axis=3, concat_axis=0, tiled=True)]
    select_n x6 -> x0, other arithmetic: 9.22 us -> none  [the longest x1 5.41 us: local(): altered = jnp.where(placed[:, :, None, None], base_rows[:, None], channels)]
  transfers between devices with their start and end apart: 3 -> 0, of which waited for: 1 -> 0; matrix products, arithmetic and copies ran while one was open for 29% -> 0% of each run, Pallas kernels for 0% -> 0%
where the time goes in v1:
time: 71.3 us; the launch traced here: 70.6 us
  Pallas kernels  64.1 us (90%)
  local copies, waits for them, and re-layouts  6.21 us (9%)
    pallas_call x1, Pallas kernels, local(): pl.pallas_call(functools.partial(kernel, n_var, n_tp, chunks, width), out...  64.1 us
    unnamed x14, local copies, waits for them, and re-layouts  4.33 us

profile of v1, /device:TPU:0, one launch (start us, length us, event | category | flops | bytes accessed | tf_op | source)
XLA Modules:
  0.0 70.6 jit_solution(6303814246955924874)
XLA Ops:
  0.0 0.7 broadcast_in_dim.3
  0.7 0.9 %copy.13 = bf16[128,128]{0,1:T(8,128)(2,1)S(1)} copy(bf16[128,128]{1,0:T(8,128)(2,1)} %param.15) | data formatting | bytes 65536 | tf_op args[4]
  1.6 0.1 rev.3
  1.7 0.8 %copy.14 = bf16[4,3,2048]{2,1,0:T(4,128)(2,1)S(1)} copy(bf16[4,3,2048]{2,0,1:T(4,128)(2,1)} %param.17) | data formatting | bytes 98304 | tf_op args[6]
  2.5 0.9 %pad_bitcast_fusion = bf16[24,2048]{1,0:T(8,128)(2,1)S(1)} fusion(bf16[3,7,2048]{2,1,0:T(8,128)(2,1)} %bitcast.12), kind=kLoop, calls=%fused_computation.6 | loop fusion | bytes 184320 | tf_op jit(solution)/shard_map/reshape | solution.py:296
  3.4 0.0 copy-start
  3.4 0.0 copy-start.1
  3.5 0.0 copy-start.2
  3.5 0.0 copy-start.3
  3.5 0.0 copy-start.4
  3.5 1.6 %copy.16 = bf16[6,6,3,2048]{3,1,2,0:T(8,128)(2,1)S(1)} copy(bf16[6,6,3,2048]{3,2,1,0:T(4,128)(2,1)} %param.13) | data formatting | bytes 884736 | tf_op args[2]
  5.1 0.2 pad.18
  5.3 0.1 pad_maximum_fusion.lead
  5.4 0.1 copy-done
  5.5 0.0 copy-done.1
  5.5 0.0 copy-done.2
  5.5 0.0 copy-done.3
  5.5 0.0 copy-done.4
  5.5 64.1 %shard_map.109 = bf16[2,32,8192]{2,1,0:T(8,128)(2,1)S(1)} custom-call(s32[64]{0:T(128)S(1)} %bitcast.10, s32[64]{0:T(128)S(1)} %copy-done.2, s32[8]{0:T(128)S(1)} %copy-done.3, s32[8]{0:T(128)S(1)} %copy-done.4, bf16[6,127,2048]{2,1,0:T(8,128)(2,1)S(1)} %copy-done, bf16[6,3,16,2048]{3,2,1,0:T(8,128)(2,1)S(1)} %pad_maximum_fusion.lead, ...), custom_call_target="tpu_custom_call" | custom-call | flops 6000000000 | bytes 12000000 | tf_op jit(solution)/shard_map/pallas_call | solution.py:304
  69.6 1.0 %copy.18 = bf16[2,32,8192]{2,1,0:T(8,128)(2,1)} copy(bf16[2,32,8192]{2,1,0:T(8,128)(2,1)S(1)} %shard_map.109) | data formatting | bytes 2097152
  (2 shorter events, 0.0 us)
Async XLA Ops:
  3.4 2.1 %copy-start = (bf16[6,127,2048]{2,1,0:T(8,128)(2,1)S(1)}, bf16[6,127,2048]{2,1,0:T(8,128)(2,1)}, u32[]{:S(2)}) copy-start(bf16[6,127,2048]{2,1,0:T(8,128)(2,1)} %hist.1) | copy-start | bytes 9363460
  3.4 2.1 %copy-start.1 = (s32[64,1]{0,1:T(1,128)S(1)}, s32[64,1]{0,1:T(1,128)}, u32[]{:S(2)}) copy-start(s32[64,1]{0,1:T(1,128)} %param.18) | copy-start | bytes 772
  3.5 2.1 %copy-start.2 = (s32[64]{0:T(128)S(1)}, s32[64]{0:T(128)}, u32[]{:S(2)}) copy-start(s32[64]{0:T(128)} %slot.1) | copy-start | bytes 772
  3.5 2.0 %copy-start.3 = (s32[8]{0:T(128)S(1)}, s32[8]{0:T(128)}, u32[]{:S(2)}) copy-start(s32[8]{0:T(128)} %pos.1) | copy-start | bytes 100
  3.5 2.0 %copy-start.4 = (s32[8]{0:T(128)S(1)}, s32[8]{0:T(128)}, u32[]{:S(2)}) copy-start(s32[8]{0:T(128)} %allele.1) | copy-start | bytes 100
